TPU v7x, 32 devices: a whole 2x2x4 slice. The times are simulated.
32 devices in a mesh: pipe: 4 (over y, x), dp: 8 (over z, core).
Axes of the slice: x: 2, y: 2, z: 4, core: 2. Of those that a mesh axis runs over, the one named last changes fastest.
Arguments:
- grad_out: bfloat16 [4, 2, 2, 32, 3584], P('pipe', None, None, 'dp'), may hold values from -6 to 6
- hidden: bfloat16 [4, 2, 2, 32, 9216], P('pipe', None, None, None, 'dp'), may hold values from -5 to 5
- weights: bfloat16 [4, 9216, 3584], P('pipe', 'dp'), may hold values from -5 to 5
- counts: int32 [4, 2, 2, 8], P('pipe', None, None, 'dp'), may hold values from 1 to 4
Outputs:
- grad_hidden: bfloat16 [4, 2, 2, 32, 9216], P('pipe', None, None, None, 'dp')
- new_weights: bfloat16 [4, 9216, 3584], P('pipe', 'dp')
All inputs are finite; a program needn't handle non-finite values.
Results may differ from a plain program's by a relative error of at most 0.0034.
Values may be sent and summed in bfloat16 or wider, within the bound.
A program may use at most 64 MiB of HBM per device.

v0:
```python
import jax
import jax.numpy as jnp
from jax import lax
from jax.sharding import PartitionSpec as P

step_rate = 2.0


def from_partner(block, axis, apart):
    count = lax.axis_size(axis)
    route = []
    for low in range(count):
        high = low | 1 << apart
        if high != low and high < count:
            route += [(low, high), (high, low)]
    return lax.ppermute(block, axis, route)


def shards(grad_out, hidden, weights, counts):
    row_total = grad_out.shape[3]
    full_width = grad_out.shape[4]
    micro = hidden.shape[2]
    group_rows = hidden.shape[3]
    share = hidden.shape[4]
    scale_factor = float(full_width) ** (-0.5)
    slot_index = lax.broadcasted_iota(jnp.int32, (1, 1, 1, row_total), 3)
    live_rows = slot_index < counts
    masked = jnp.where(live_rows[..., None], grad_out, jnp.zeros_like(grad_out))
    own_weight = weights[0]
    pipe_bits = lax.axis_size("pipe").bit_length() - 1
    outgoing = jnp.concatenate(
        [masked[0, 1].reshape(micro, -1), hidden[0, 1].reshape(micro, -1)], axis=1
    )
    incoming = outgoing
    for fetch_bit_index in range(pipe_bits):
        incoming = from_partner(incoming, "pipe", fetch_bit_index)
    split_at = row_total * full_width
    mirror_masked = incoming[:, :split_at].reshape(micro, row_total, full_width)
    mirror_hidden = incoming[:, split_at:].reshape(micro, group_rows, share)
    mirror_masked, mirror_hidden = (mirror_masked, mirror_hidden)
    both_masked = jnp.stack([masked[0, 0], mirror_masked], axis=0)
    both_hidden = jnp.stack([hidden[0, 0], mirror_hidden], axis=0)
    piece = lax.all_gather(both_masked, "dp", axis=2, tiled=True)
    rows_out = jnp.einsum("rmkd,hd->rmkh", piece, own_weight, preferred_element_type=jnp.float32)
    grad_acc = rows_out
    weight_acc = jnp.einsum(
        "rmkh,rmkd->rhd", both_hidden, piece, preferred_element_type=jnp.float32
    )
    grad_acc, weight_acc = (grad_acc, weight_acc)
    grad_rows = (grad_acc * scale_factor).astype(jnp.bfloat16)
    partial_value = (weight_acc * scale_factor).astype(jnp.bfloat16)
    gradient = partial_value[0].astype(jnp.float32) + partial_value[1].astype(jnp.float32)
    new_weight = (own_weight.astype(jnp.float32) - step_rate * gradient).astype(jnp.bfloat16)
    returned = grad_rows[1]
    for bit_index in range(pipe_bits):
        returned = from_partner(returned, "pipe", bit_index)
    grad_hidden = jnp.stack([grad_rows[0], returned], axis=0)[None]
    return (grad_hidden, new_weight[None])


def solution(mesh):
    return jax.shard_map(
        shards,
        mesh=mesh,
        in_specs=(
            P("pipe", None, None, "dp", None),
            P("pipe", None, None, None, "dp"),
            P("pipe", "dp", None),
            P("pipe", None, None, "dp"),
        ),
        out_specs=(P("pipe", None, None, None, "dp"), P("pipe", "dp", None)),
        check_vma=False,
    )
```

profile of v0, /device:TPU:0, one launch (start us, length us, event | category | flops | bytes accessed | tf_op | source)
XLA Modules:
  0.0 65.1 jit_solution(16177197494422398560)
XLA Ops:
  0.6 0.7 %iota_compare_fusion = pred[2,2,4]{1,2,0:T(4,128)(4,1)S(1)} fusion(s32[2,2]{1,0:T(2,128)} %bitcast.42), kind=kLoop, calls=%fused_computation.21 | loop fusion | flops 16 | bytes 32 | tf_op jit(solution)/shard_map/lt | solution.py:27
  1.3 1.1 %broadcast_select_fusion = bf16[1,2,2,4,3584]{4,2,3,1,0:T(2,128)(2,1)S(1)} fusion(pred[2,2,4]{1,2,0:T(4,128)(4,1)S(1)} %iota_compare_fusion, bf16[1,2,2,4,3584]{4,3,2,1,0:T(4,128)(2,1)} %param.4), kind=kLoop, calls=%fused_computation.13 | loop fusion | flops 57344 | bytes 229392 | tf_op jit(solution)/shard_map/jit(_where)/select_n | solution.py:28
  2.4 0.1 slice_bitcast_fusion.3
  2.5 1.0 %slice_bitcast_fusion.1 = (bf16[1,2,32,1152]{3,2,1,0:T(8,128)(2,1)S(1)}, bf16[1,2,32,1152]{3,2,1,0:T(8,128)(2,1)S(1)}) fusion(bf16[1,2,2,32,1152]{4,3,2,1,0:T(8,128)(2,1)} %param.5), kind=kLoop, calls=%fused_computation.17 | loop fusion | bytes 589824 | tf_op jit(solution)/shard_map/stack;squeeze | solution.py:42
  3.5 0.1 copy.11
  3.6 0.2 pad_maximum_fusion
  3.8 3.0 %collective-permute-start = (bf16[2,51200]{1,0:T(2,128)(2,1)S(1)}, bf16[2,51200]{1,0:T(2,128)(2,1)S(1)}, u32[]{:S(2)}, u32[]{:S(2)}) collective-permute-start(bf16[2,51200]{1,0:T(2,128)(2,1)S(1)} %pad_maximum_fusion), channel_id=1, source_target_pairs={{0,8},{8,0},{16,24},{24,16},{1,9},{9,1},{17,25},{25,17},{2,10},{10... | collective-permute-start | bytes 614408 | tf_op jit(solution)/shard_map/ppermute | solution.py:16
  6.8 5.1 %collective-permute-done = bf16[2,51200]{1,0:T(2,128)(2,1)S(1)} collective-permute-done((bf16[2,51200]{1,0:T(2,128)(2,1)S(1)}, bf16[2,51200]{1,0:T(2,128)(2,1)S(1)}, u32[]{:S(2)}, u32[]{:S(2)}) %collective-permute-start) | collective-permute-done | bytes 204832 | tf_op jit(solution)/shard_map/ppermute | solution.py:16
  11.9 1.8 %collective-permute-start.1 = (bf16[2,51200]{1,0:T(2,128)(2,1)S(1)}, bf16[2,51200]{1,0:T(2,128)(2,1)S(1)}, u32[]{:S(2)}, u32[]{:S(2)}) collective-permute-start(bf16[2,51200]{1,0:T(2,128)(2,1)S(1)} %collective-permute-done), channel_id=1, source_target_pairs={{0,16},{16,0},{8,24},{24,8},{1,17},{17,1},{9,25},{25,9},{2,18},{18... | collective-permute-start | bytes 614408 | tf_op jit(solution)/shard_map/ppermute | solution.py:16
  13.6 4.5 %collective-permute-done.1 = bf16[2,51200]{1,0:T(2,128)(2,1)S(1)} collective-permute-done((bf16[2,51200]{1,0:T(2,128)(2,1)S(1)}, bf16[2,51200]{1,0:T(2,128)(2,1)S(1)}, u32[]{:S(2)}, u32[]{:S(2)}) %collective-permute-start.1) | collective-permute-done | bytes 204832 | tf_op jit(solution)/shard_map/ppermute | solution.py:16
  18.1 0.1 slice.45
  18.3 0.2 pad_maximum_fusion.1
  18.5 16.7 %all_gather.3 = bf16[2,2,32,3584]{3,1,0,2:T(2,128)(2,1)S(1)} all-gather(bf16[2,2,4,3584]{3,1,0,2:T(2,128)(2,1)S(1)} %pad_maximum_fusion.1), channel_id=1, replica_groups=mesh['pipe'=4,'dp'=8] {'dp'}, dimensions={2}, use_global_device_ids=true | all-gather | bytes 1032192 | tf_op jit(solution)/shard_map/all_gather | solution.py:43
  35.2 6.0 %fusion.6 = bf16[2,2,32,1152]{3,2,1,0:T(8,128)(2,1)S(1)} fusion(bf16[1,1152,3584]{2,1,0:T(8,128)(2,1)} %param.6, bf16[2,2,32,3584]{3,1,0,2:T(2,128)(2,1)S(1)} %all_gather.3), kind=kOutput, calls=%fused_computation.6 | convolution fusion | flops 1057259520 | bytes 9469952 | tf_op jit(solution)/shard_map/rmkd,hd->rmkh/dot_general | solution.py:44
  41.3 1.6 %collective-permute-start.2 = (bf16[2,32,1152]{2,1,0:T(8,128)(2,1)S(1)}, bf16[2,32,1152]{2,1,0:T(8,128)(2,1)S(1)}, u32[]{:S(2)}, u32[]{:S(2)}) collective-permute-start(bf16[2,32,1152]{2,1,0:T(8,128)(2,1)S(1)} %get-tuple-element.5), channel_id=1, source_target_pairs={{0,8},{8,0},{16,24},{24,16},{1,9},{9,1},{17,25},{25,17},{2,10},{10... | collective-permute-start | bytes 442376 | tf_op jit(solution)/shard_map/ppermute | solution.py:16
  42.8 8.0 %fusion = bf16[2,1152,3584]{2,1,0:T(8,128)(2,1)} fusion(bf16[2,2,32,3584]{3,1,0,2:T(2,128)(2,1)S(1)} %all_gather.3, bf16[1,2,32,1152]{3,2,1,0:T(8,128)(2,1)S(1)} %copy.19, bf16[1,2,32,1152]{3,2,1,0:T(8,128)(2,1)S(1)} %get-tuple-element.2), kind=kOutput, calls=%fused_computation.1 | convolution fusion | flops 1073627136 | bytes 17727488 | tf_op jit(solution)/shard_map/rmkh,rmkd->rhd/dot_general | solution.py:46
  50.8 0.0 collective-permute-done.2
  50.8 1.5 %collective-permute-start.3 = (bf16[2,32,1152]{2,1,0:T(8,128)(2,1)S(1)}, bf16[2,32,1152]{2,1,0:T(8,128)(2,1)S(1)}, u32[]{:S(2)}, u32[]{:S(2)}) collective-permute-start(bf16[2,32,1152]{2,1,0:T(8,128)(2,1)S(1)} %collective-permute-done.2), channel_id=1, source_target_pairs={{0,16},{16,0},{8,24},{24,8},{1,17},{17,1},{9,25},{25,9},{2,18},{18... | collective-permute-start | bytes 442376 | tf_op jit(solution)/shard_map/ppermute | solution.py:16
  52.4 12.0 %subtract_convert_fusion = bf16[1,1152,3584]{2,1,0:T(8,128)(2,1)} fusion(bf16[1,1152,3584]{2,1,0:T(8,128)(2,1)} %param.6, bf16[2,1152,3584]{2,1,0:T(8,128)(2,1)} %fusion), kind=kLoop, calls=%fused_computation.2 | loop fusion | flops 28901376 | bytes 33030144 | tf_op jit(solution)/shard_map/convert_element_type | solution.py:53
  64.4 0.0 collective-permute-done.3
  64.4 0.7 %maximum_bitcast_fusion = bf16[1,2,2,32,1152]{4,3,2,1,0:T(8,128)(2,1)} fusion(bf16[1,2,32,1152]{3,2,1,0:T(8,128)(2,1)S(1)} %bitcast.41, bf16[1,2,32,1152]{3,2,1,0:T(8,128)(2,1)S(1)} %get-tuple-element.4), kind=kLoop, calls=%fused_computation.9 | loop fusion | flops 147456 | bytes 589824 | tf_op jit(solution)/shard_map/broadcast_in_dim | solution.py:57
  (3 shorter events, 0.1 us)
Async XLA Ops:
  3.8 8.1 %collective-permute-start = (bf16[2,51200]{1,0:T(2,128)(2,1)S(1)}, bf16[2,51200]{1,0:T(2,128)(2,1)S(1)}, u32[]{:S(2)}, u32[]{:S(2)}) collective-permute-start(bf16[2,51200]{1,0:T(2,128)(2,1)S(1)} %pad_maximum_fusion), channel_id=1, source_target_pairs={{0,8},{8,0},{16,24},{24,16},{1,9},{9,1},{17,25},{25,17},{2,10},{10... | collective-permute-start | bytes 614408 | tf_op jit(solution)/shard_map/ppermute | solution.py:16
  11.9 6.3 %collective-permute-start.1 = (bf16[2,51200]{1,0:T(2,128)(2,1)S(1)}, bf16[2,51200]{1,0:T(2,128)(2,1)S(1)}, u32[]{:S(2)}, u32[]{:S(2)}) collective-permute-start(bf16[2,51200]{1,0:T(2,128)(2,1)S(1)} %collective-permute-done), channel_id=1, source_target_pairs={{0,16},{16,0},{8,24},{24,8},{1,17},{17,1},{9,25},{25,9},{2,18},{18... | collective-permute-start | bytes 614408 | tf_op jit(solution)/shard_map/ppermute | solution.py:16
  41.3 9.6 %collective-permute-start.2 = (bf16[2,32,1152]{2,1,0:T(8,128)(2,1)S(1)}, bf16[2,32,1152]{2,1,0:T(8,128)(2,1)S(1)}, u32[]{:S(2)}, u32[]{:S(2)}) collective-permute-start(bf16[2,32,1152]{2,1,0:T(8,128)(2,1)S(1)} %get-tuple-element.5), channel_id=1, source_target_pairs={{0,8},{8,0},{16,24},{24,16},{1,9},{9,1},{17,25},{25,17},{2,10},{10... | collective-permute-start | bytes 442376 | tf_op jit(solution)/shard_map/ppermute | solution.py:16
  50.8 13.6 %collective-permute-start.3 = (bf16[2,32,1152]{2,1,0:T(8,128)(2,1)S(1)}, bf16[2,32,1152]{2,1,0:T(8,128)(2,1)S(1)}, u32[]{:S(2)}, u32[]{:S(2)}) collective-permute-start(bf16[2,32,1152]{2,1,0:T(8,128)(2,1)S(1)} %collective-permute-done.2), channel_id=1, source_target_pairs={{0,16},{16,0},{8,24},{24,8},{1,17},{17,1},{9,25},{25,9},{2,18},{18... | collective-permute-start | bytes 442376 | tf_op jit(solution)/shard_map/ppermute | solution.py:16
where the time goes:
time: 65.4 us; the launch traced here: 65.1 us
  blocking collectives  16.7 us (26%)
  other arithmetic  14.9 us (23%)
  matrix products  14.1 us (22%)
  waiting for transfers between devices  9.58 us (15%)
  starting transfers between devices  7.85 us (12%)
  local copies, waits for them, and re-layouts  1.39 us (2%)
  between operations  0.71 us (1%)
    all_gather x1, blocking collectives, shards(): piece = lax.all_gather(both_masked, 'dp', axis=2, tiled=True)  16.7 us
    convert_element_type x1, other arithmetic, shards(): (own_weight.astype(jnp.float32) - step_rate * gradient).astype(jnp.bfloat16)  12 us
    ppermute x4, waiting for transfers between devices, from_partner(): return lax.ppermute(block, axis, route)  9.58 us
    dot_general x1, matrix products, shards(): jnp.einsum('rmkh,rmkd->rhd', both_hidden, piece, preferred_element_type=j...  8.02 us
    ppermute x4, starting transfers between devices, from_partner(): return lax.ppermute(block, axis, route)  7.85 us
    dot_general x1, matrix products, shards(): jnp.einsum('rmkd,hd->rmkh', piece, own_weight, preferred_element_type=jnp...  6.04 us
  transfers between devices with their start and end apart: 4, of which 2 were waited for; matrix products, arithmetic and copies ran while one was open for 31% of the time, Pallas kernels for 0%

commit v1 on v0

v1 whole, which is shorter than its diff:
```python
import functools

import jax
import jax.numpy as jnp
from jax import lax
from jax.experimental import pallas as pl
from jax.experimental.pallas import tpu as pltpu
from jax.sharding import PartitionSpec as P

step_rate = 2.0
MESH = pl.DeviceIdType.MESH
LEFT, RIGHT, SIBLING = 0, 1, 2


def when(condition, action):
    if condition is True:
        action()
    else:
        pl.when(condition)(action)


def gather_kernel(
    n_pipe, n_dp, scale_factor, chunk,
    counts_ref, grad_ref, hidden_ref, weights_ref,
    rows_ref, acts_ref, out_ref,
    staged, own_slot1, own_weight, own_hidden, mirror_hidden, ret,
    send_sem, recv_sem, pair_send, pair_recv, ret_send, ret_recv, load_sem,
):
    p = lax.axis_index("pipe")
    k = lax.axis_index("dp")
    z = k // 2
    n = n_dp // 2
    mirror = (n_pipe - 1 - p, k)
    sibling = k + 1 - 2 * (k % 2)
    has_left = z > 0
    has_right = z < n - 1
    micro, row_total, width = grad_ref.shape[2], grad_ref.shape[3], grad_ref.shape[4]
    half = width // 2
    block_rows = micro * row_total
    group_rows = hidden_ref.shape[3]
    share = hidden_ref.shape[4]

    load_hidden = pltpu.make_async_copy(hidden_ref.at[0], own_hidden, load_sem.at[0])
    load_weight = pltpu.make_async_copy(weights_ref.at[0], own_weight, load_sem.at[1])
    load_hidden.start()
    load_weight.start()

    barrier = pltpu.get_barrier_semaphore()
    pl.semaphore_signal(barrier, inc=1, device_id=mirror, device_id_type=MESH)
    pl.semaphore_signal(barrier, inc=1, device_id=(p, sibling), device_id_type=MESH)

    @pl.when(has_left)
    def _():
        pl.semaphore_signal(barrier, inc=1, device_id=(p, k - 2), device_id_type=MESH)

    @pl.when(has_right)
    def _():
        pl.semaphore_signal(barrier, inc=1, device_id=(p, k + 2), device_id_type=MESH)

    slot_index = lax.broadcasted_iota(jnp.int32, (row_total, width), 0)
    for r in (1, 0):
        for m in range(micro):
            live = slot_index < counts_ref[0, r, m, 0]
            rows = jnp.where(live, grad_ref[0, r, m].astype(jnp.float32), 0.0)
            for h in range(2):
                staged[r, pl.ds(h * block_rows + m * row_total, row_total), :] = rows[:, h * half:(h + 1) * half]
        packed = staged[r].astype(jnp.bfloat16)
        if r == 1:
            own_slot1[...] = packed
        else:
            rows_ref[0, k] = packed

    pl.semaphore_wait(barrier, 2 + has_left.astype(jnp.int32) + has_right.astype(jnp.int32))

    def hop(s, origin, way):
        target = {LEFT: k - 2, RIGHT: k + 2, SIBLING: sibling}[way]
        return pltpu.make_async_remote_copy(
            src_ref=rows_ref.at[s, origin],
            dst_ref=rows_ref.at[s, origin],
            send_sem=send_sem.at[s, origin, way],
            recv_sem=recv_sem.at[s, origin],
            device_id=(p, target),
            device_id_type=MESH,
        )

    def arrived(s, origin):
        hop(s, origin, SIBLING).wait_recv()

    mirror_rows = pltpu.make_async_remote_copy(
        src_ref=own_slot1, dst_ref=rows_ref.at[1, k],
        send_sem=pair_send.at[0], recv_sem=recv_sem.at[1, k],
        device_id=mirror, device_id_type=MESH,
    )
    mirror_acts = pltpu.make_async_remote_copy(
        src_ref=own_hidden.at[1], dst_ref=mirror_hidden,
        send_sem=pair_send.at[1], recv_sem=pair_recv.at[1],
        device_id=mirror, device_id_type=MESH,
    )

    sent = []

    def send(s, origin, way, condition):
        sent.append((s, origin, way, condition))
        when(condition, lambda: hop(s, origin, way).start())

    def send_own(s):
        send(s, k, LEFT, has_left)
        send(s, k, RIGHT, has_right)
        send(s, k, SIBLING, True)

    def relay(s, j):
        from_left = z >= j
        from_right = z + j < n
        left_origin = jnp.maximum(k - 2 * j, 0)
        right_origin = jnp.minimum(k + 2 * j, n_dp - 1)
        pl.when(from_left)(lambda: arrived(s, left_origin))
        send(s, left_origin, RIGHT, jnp.logical_and(from_left, has_right))
        send(s, left_origin, SIBLING, from_left)
        pl.when(from_right)(lambda: arrived(s, right_origin))
        send(s, right_origin, LEFT, jnp.logical_and(from_right, has_left))
        send(s, right_origin, SIBLING, from_right)

    mirror_rows.start()
    send_own(0)
    load_hidden.wait()
    mirror_acts.start()
    arrived(1, k)
    send_own(1)
    for j in range(1, n - 1):
        relay(0, j)
        relay(1, j)

    mirror_acts.wait_recv()
    tokens = micro * group_rows
    gathered = n_dp * 2 * block_rows
    at_row = lax.broadcasted_iota(jnp.int32, (gathered, tokens), 0)
    at_token = lax.broadcasted_iota(jnp.int32, (gathered, tokens), 1)
    rank, inside = at_row // (2 * block_rows), at_row % (2 * block_rows)
    which_half, inside = inside // block_rows, inside % block_rows
    wanted = (inside // row_total) * group_rows + rank * row_total + inside % row_total
    for h in range(2):
        place = jnp.where((wanted == at_token) & (which_half == h), 1.0, 0.0).astype(jnp.bfloat16)
        for s in range(2):
            acts = (own_hidden[0] if s == 0 else mirror_hidden[...]).reshape(tokens, share)
            acts_ref[h, :, pl.ds(s * gathered, gathered)] = lax.dot_general(
                acts, place, (((0,), (1,)), ((), ())), preferred_element_type=jnp.float32
            ).astype(jnp.bfloat16)

    if n > 1:
        relay(0, n - 1)
        relay(1, n - 1)
    load_weight.wait()

    out_token = lax.broadcasted_iota(jnp.int32, (tokens, tokens), 0)
    in_token = lax.broadcasted_iota(jnp.int32, (tokens, tokens), 1)
    out_m, out_t = out_token // group_rows, out_token % group_rows
    source = (out_t // row_total) * block_rows + out_m * row_total + out_t % row_total
    unplace = jnp.where(source == in_token, 1.0, 0.0).astype(jnp.bfloat16)

    def product(s, c):
        rows = rows_ref[s].reshape(gathered, half)
        parts = []
        for h in range(2):
            part = lax.dot_general(
                rows, own_weight[pl.ds(c * chunk, chunk), pl.ds(h * half, half)],
                (((1,), (1,)), ((), ())), preferred_element_type=jnp.float32,
            ).reshape(n_dp, 2, block_rows, chunk)
            parts.append(part[:, h])
        total = ((parts[0] + parts[1]) * scale_factor).astype(jnp.bfloat16).astype(jnp.float32)
        total = total.reshape(tokens, chunk).astype(jnp.bfloat16)
        return jnp.dot(unplace, total, preferred_element_type=jnp.float32).astype(
            jnp.bfloat16
        ).reshape(micro, group_rows, chunk)

    def give_back(c):
        columns = pl.ds(c * chunk, chunk)
        return pltpu.make_async_remote_copy(
            src_ref=ret.at[:, :, columns], dst_ref=out_ref.at[0, 1, :, :, columns],
            send_sem=ret_send.at[c], recv_sem=ret_recv.at[c],
            device_id=mirror, device_id_type=MESH,
        )

    for s in (1, 0):
        for j in range(n):
            for origin, there in ((sibling - 2 * j, z >= j), (sibling + 2 * j, z + j < n)):
                if j == 0 and origin is not None and there is not None:
                    pass
                safe = jnp.clip(origin, 0, n_dp - 1)
                if j == 0:
                    arrived(s, sibling)
                    break
                pl.when(there)(functools.partial(arrived, s, safe))
        for c in range(share // chunk):
            value = product(s, c)
            if s == 1:
                ret[:, :, pl.ds(c * chunk, chunk)] = value
                give_back(c).start()
            else:
                out_ref[0, 0, :, :, pl.ds(c * chunk, chunk)] = value

    mirror_rows.wait_send()
    mirror_acts.wait_send()
    for s, origin, way, condition in sent:
        when(condition, functools.partial(lambda *a: hop(*a).wait_send(), s, origin, way))
    for c in range(share // chunk):
        give_back(c).wait()


def update_kernel(factor, weights_ref, acts_ref, rows_ref, new_ref):
    half = rows_ref.shape[1]
    for h in range(2):
        columns = pl.ds(h * half, half)
        total = jnp.dot(acts_ref[h], rows_ref[...], preferred_element_type=jnp.float32)
        new_ref[0, :, columns] = (
            weights_ref[0, :, columns].astype(jnp.float32) - factor * total
        ).astype(jnp.bfloat16)


def shards(n_pipe, n_dp, grad_out, hidden, weights, counts):
    _, _, micro, row_total, width = grad_out.shape
    group_rows, share = hidden.shape[3], hidden.shape[4]
    block = 2 * micro * row_total
    half = width // 2
    gathered = n_dp * block
    scale_factor = float(width) ** (-0.5)
    chunk = 384 if share % 384 == 0 else share
    step = max(b for b in range(16, 193, 16) if share % b == 0)
    vmem = pl.BlockSpec(memory_space=pltpu.VMEM)
    hbm = pl.BlockSpec(memory_space=pl.ANY)
    rows, acts, grad_hidden = pl.pallas_call(
        functools.partial(gather_kernel, n_pipe, n_dp, scale_factor, chunk),
        out_shape=(
            jax.ShapeDtypeStruct((2, n_dp, block, half), jnp.bfloat16),
            jax.ShapeDtypeStruct((2, share, 2 * gathered), jnp.bfloat16),
            jax.ShapeDtypeStruct(hidden.shape, jnp.bfloat16),
        ),
        in_specs=[pl.BlockSpec(memory_space=pltpu.SMEM), vmem, hbm, hbm],
        out_specs=(vmem, vmem, vmem),
        scratch_shapes=[
            pltpu.VMEM((2, block, half), jnp.float32),
            pltpu.VMEM((block, half), jnp.bfloat16),
            pltpu.VMEM((share, width), jnp.bfloat16),
            pltpu.VMEM((2, micro, group_rows, share), jnp.bfloat16),
            pltpu.VMEM((micro, group_rows, share), jnp.bfloat16),
            pltpu.VMEM((micro, group_rows, share), jnp.bfloat16),
            pltpu.SemaphoreType.DMA((2, n_dp, 3)),
            pltpu.SemaphoreType.DMA((2, n_dp)),
            pltpu.SemaphoreType.DMA((2,)),
            pltpu.SemaphoreType.DMA((2,)),
            pltpu.SemaphoreType.DMA((share // chunk,)),
            pltpu.SemaphoreType.DMA((share // chunk,)),
            pltpu.SemaphoreType.DMA((2,)),
        ],
        compiler_params=pltpu.CompilerParams(
            collective_id=0, has_side_effects=True, vmem_limit_bytes=36 * 2**20
        ),
        name="gather",
    )(counts, grad_out, hidden, weights)
    new_weights = pl.pallas_call(
        functools.partial(update_kernel, step_rate * scale_factor),
        grid=(share // step,),
        out_shape=jax.ShapeDtypeStruct(weights.shape, jnp.bfloat16),
        in_specs=[
            pl.BlockSpec((1, step, width), lambda i: (0, i, 0)),
            pl.BlockSpec((2, step, 2 * gathered), lambda i: (0, i, 0)),
            pl.BlockSpec((2 * gathered, half), lambda i: (0, 0)),
        ],
        out_specs=pl.BlockSpec((1, step, width), lambda i: (0, i, 0)),
        compiler_params=pltpu.CompilerParams(vmem_limit_bytes=24 * 2**20),
        name="update",
    )(weights, acts, rows.reshape(2 * gathered, half))
    return grad_hidden, new_weights


def solution(mesh):
    return jax.shard_map(
        functools.partial(shards, mesh.shape["pipe"], mesh.shape["dp"]),
        mesh=mesh,
        in_specs=(
            P("pipe", None, None, "dp", None),
            P("pipe", None, None, None, "dp"),
            P("pipe", "dp", None),
            P("pipe", None, None, "dp"),
        ),
        out_specs=(P("pipe", None, None, None, "dp"), P("pipe", "dp", None)),
        check_vma=False,
    )
```

time: 65.4 us -> 41.3 us (0.63)
  Pallas kernels: 0 us -> 33.7 us
  blocking collectives: 16.7 us -> 0 us
  other arithmetic: 14.9 us -> 0 us
  matrix products: 14.1 us -> 0 us
  waiting for transfers between devices: 9.58 us -> 0 us
  starting transfers between devices: 7.85 us -> 0 us
  local copies, waits for them, and re-layouts: 1.39 us -> 6.69 us
    pallas_call x0 -> x2, Pallas kernels: none -> 33.7 us  [the longest x1 28.2 us: shards(): pl.pallas_call(functools.partial(gather_kernel, n_pipe, n_dp, scale_facto...]
    all_gather x1 -> x0, blocking collectives: 16.7 us -> none  [shards(): piece = lax.all_gather(both_masked, 'dp', axis=2, tiled=True)]
    dot_general x2 -> x0, matrix products: 14.1 us -> none  [the longest x1 8.02 us: shards(): jnp.einsum('rmkh,rmkd->rhd', both_hidden, piece, preferred_element_type=j...]
    convert_element_type x1 -> x0, other arithmetic: 12 us -> none  [shards(): (own_weight.astype(jnp.float32) - step_rate * gradient).astype(jnp.bfloat16)]
    ppermute x4 -> x0, waiting for transfers between devices: 9.58 us -> none  [from_partner(): return lax.ppermute(block, axis, route)]
    ppermute x4 -> x0, starting transfers between devices: 7.85 us -> none  [from_partner(): return lax.ppermute(block, axis, route)]
    unnamed x2 -> x8, local copies, waits for them, and re-layouts: 0.13 us -> 6.69 us
    another operation x2 -> x0, local copies, waits for them, and re-layouts: 1.09 us -> none  [the longest x1 1.01 us: shards(): both_hidden = jnp.stack([hidden[0, 0], mirror_hidden], axis=0)]
  transfers between devices with their start and end apart: 4 -> 0, of which waited for: 2 -> 0; matrix products, arithmetic and copies ran while one was open for 31% -> 0% of each run, Pallas kernels for 0% -> 0%
where the time goes in v1:
time: 41.3 us; the launch traced here: 41.1 us
  Pallas kernels  33.7 us (82%)
  local copies, waits for them, and re-layouts  6.69 us (16%)
  between operations  0.64 us (2%)
    pallas_call x1, Pallas kernels, shards(): pl.pallas_call(functools.partial(gather_kernel, n_pipe, n_dp, scale_facto...  28.2 us
    unnamed x8, local copies, waits for them, and re-layouts  6.69 us
    pallas_call x1, Pallas kernels, shards(): pl.pallas_call(functools.partial(update_kernel, step_rate * scale_factor)...  5.53 us

profile of v1, /device:TPU:0, one launch (start us, length us, event | category | flops | bytes accessed | tf_op | source)
XLA Modules:
  0.0 41.1 jit_solution(6425860340837777200)
XLA Ops:
  0.6 0.8 %copy.6.counts_ref = s32[1,2,2,1]{3,2,1,0:T(2,128)S(1)} copy(s32[1,2,2,1]{2,3,1,0:T(1,128)} %param.7) | data formatting | bytes 32 | tf_op args[3]
  1.4 0.0 copy-start
  1.4 3.3 %copy-done = bf16[1,1152,3584]{2,1,0:T(8,128)(2,1)S(1)} copy-done((bf16[1,1152,3584]{2,1,0:T(8,128)(2,1)S(1)}, bf16[1,1152,3584]{2,1,0:T(8,128)(2,1)}, u32[]{:S(2)}) %copy-start) | copy-done | bytes 8257560
  4.7 0.0 copy-start.1
  4.7 1.0 %copy-done.1 = bf16[1,2,2,32,1152]{4,3,2,1,0:T(8,128)(2,1)S(1)} copy-done((bf16[1,2,2,32,1152]{4,3,2,1,0:T(8,128)(2,1)S(1)}, bf16[1,2,2,32,1152]{4,3,2,1,0:T(8,128)(2,1)}, u32[]{:S(2)}) %copy-start.1) | copy-done | bytes 294936
  5.7 0.0 copy-start.2
  5.7 0.9 %copy-done.2 = bf16[1,2,2,4,3584]{4,3,2,1,0:T(4,128)(2,1)S(1)} copy-done((bf16[1,2,2,4,3584]{4,3,2,1,0:T(4,128)(2,1)S(1)}, bf16[1,2,2,4,3584]{4,3,2,1,0:T(4,128)(2,1)}, u32[]{:S(2)}) %copy-start.2) | copy-done | bytes 114712
  6.6 28.2 %gather.1 = (bf16[2,8,16,1792]{3,2,1,0:T(8,128)(2,1)S(1)}, bf16[2,1152,256]{2,1,0:T(8,128)(2,1)S(1)}, bf16[1,2,2,32,1152]{4,3,2,1,0:T(8,128)(2,1)S(1)}) custom-call(s32[1,2,2,1]{3,2,1,0:T(2,128)S(1)} %copy.6.counts_ref, bf16[1,2,2,4,3584]{4,3,2,1,0:T(4,128)(2,1)S(1)} %copy-done.2, bf16[1,2,2,32,1152]{4,3,2,1,0:T(8,128)(2,1)S(1)} %copy-done.1, ...), custom_call_target="tpu_custom_call" | custom-call | tf_op jit(solution)/shard_map/gather/pallas_call | solution.py:230
  34.8 5.5 %update.1 = bf16[1,1152,3584]{2,1,0:T(8,128)(2,1)} custom-call(bf16[1,1152,3584]{2,1,0:T(8,128)(2,1)S(1)} %copy-done, bf16[2,1152,256]{2,1,0:T(8,128)(2,1)S(1)} %get-tuple-element.6.acts_ref, bf16[256,1792]{1,0:T(8,128)(2,1)S(1)} %bitcast.1), custom_call_target="tpu_custom_call" | custom-call | tf_op jit(solution)/shard_map/update/pallas_call | solution.py:259
  40.4 0.7 %copy.8 = bf16[1,2,2,32,1152]{4,3,2,1,0:T(8,128)(2,1)} copy(bf16[1,2,2,32,1152]{4,3,2,1,0:T(8,128)(2,1)S(1)} %get-tuple-element.10) | data formatting | bytes 589824
Async XLA Ops:
  1.4 3.3 %copy-start = (bf16[1,1152,3584]{2,1,0:T(8,128)(2,1)S(1)}, bf16[1,1152,3584]{2,1,0:T(8,128)(2,1)}, u32[]{:S(2)}) copy-start(bf16[1,1152,3584]{2,1,0:T(8,128)(2,1)} %weights_ref.3) | copy-start | bytes 24772612
  4.7 1.0 %copy-start.1 = (bf16[1,2,2,32,1152]{4,3,2,1,0:T(8,128)(2,1)S(1)}, bf16[1,2,2,32,1152]{4,3,2,1,0:T(8,128)(2,1)}, u32[]{:S(2)}) copy-start(bf16[1,2,2,32,1152]{4,3,2,1,0:T(8,128)(2,1)} %hidden_ref.1) | copy-start | bytes 884740
  5.7 0.9 %copy-start.2 = (bf16[1,2,2,4,3584]{4,3,2,1,0:T(4,128)(2,1)S(1)}, bf16[1,2,2,4,3584]{4,3,2,1,0:T(4,128)(2,1)}, u32[]{:S(2)}) copy-start(bf16[1,2,2,4,3584]{4,3,2,1,0:T(4,128)(2,1)} %grad_ref.1) | copy-start | bytes 344068

commit v2 on v1

v2 whole, which is shorter than its diff:
```python
import functools

import jax
import jax.numpy as jnp
from jax import lax
from jax.experimental import pallas as pl
from jax.experimental.pallas import tpu as pltpu
from jax.sharding import PartitionSpec as P

step_rate = 2.0
MESH = pl.DeviceIdType.MESH
LEFT, RIGHT, SIBLING = 0, 1, 2


def when(condition, action):
    if condition is True:
        action()
    else:
        pl.when(condition)(action)


def gather_kernel(
    n_pipe, n_dp, scale_factor, chunk,
    counts_ref, grad_ref, hidden_ref, weights_ref,
    rows_ref, acts_ref, weight_out, out_ref,
    own_grad, staged, own_slot1, landed, acts_in, ret,
    send_sem, recv_sem, pair_send, pair_recv, ret_send, ret_recv, load_sem,
):
    p = lax.axis_index("pipe")
    k = lax.axis_index("dp")
    z = k // 2
    n = n_dp // 2
    mirror = (n_pipe - 1 - p, k)
    sibling = k + 1 - 2 * (k % 2)
    has_left = z > 0
    has_right = z < n - 1
    micro, row_total, width = grad_ref.shape[2], grad_ref.shape[3], grad_ref.shape[4]
    half = width // 2
    block_rows = micro * row_total
    group_rows = hidden_ref.shape[3]
    share = hidden_ref.shape[4]
    tokens = 2 * micro * group_rows

    load_grad = pltpu.make_async_copy(grad_ref.at[0], own_grad, load_sem.at[0])
    load_acts = pltpu.make_async_copy(hidden_ref.at[0, 0], acts_in.at[0], load_sem.at[1])
    load_weight = pltpu.make_async_copy(weights_ref.at[0], weight_out, load_sem.at[2])
    load_grad.start()

    barrier = pltpu.get_barrier_semaphore()
    pl.semaphore_signal(barrier, inc=1, device_id=mirror, device_id_type=MESH)
    pl.semaphore_signal(barrier, inc=1, device_id=(p, sibling), device_id_type=MESH)

    @pl.when(has_left)
    def _():
        pl.semaphore_signal(barrier, inc=1, device_id=(p, k - 2), device_id_type=MESH)

    @pl.when(has_right)
    def _():
        pl.semaphore_signal(barrier, inc=1, device_id=(p, k + 2), device_id_type=MESH)

    load_acts.start()
    load_weight.start()
    load_grad.wait()
    slot_index = lax.broadcasted_iota(jnp.int32, (row_total, width), 0)
    for r in (1, 0):
        for m in range(micro):
            live = slot_index < counts_ref[r, m]
            rows = jnp.where(live, own_grad[r, m].astype(jnp.float32), 0.0)
            for h in range(2):
                staged[r, pl.ds(h * block_rows + m * row_total, row_total), :] = rows[:, h * half:(h + 1) * half]
        packed = staged[r].astype(jnp.bfloat16)
        if r == 1:
            own_slot1[...] = packed
        else:
            landed[0, k] = packed

    pl.semaphore_wait(barrier, 2 + has_left.astype(jnp.int32) + has_right.astype(jnp.int32))

    def hop(s, origin, way):
        target = {LEFT: k - 2, RIGHT: k + 2, SIBLING: sibling}[way]
        return pltpu.make_async_remote_copy(
            src_ref=landed.at[s, origin],
            dst_ref=landed.at[s, origin],
            send_sem=send_sem.at[s, origin, way],
            recv_sem=recv_sem.at[s, origin],
            device_id=(p, target),
            device_id_type=MESH,
        )

    def arrived(s, origin):
        hop(s, origin, SIBLING).wait_recv()

    mirror_rows = pltpu.make_async_remote_copy(
        src_ref=own_slot1, dst_ref=landed.at[1, k],
        send_sem=pair_send.at[0], recv_sem=recv_sem.at[1, k],
        device_id=mirror, device_id_type=MESH,
    )
    mirror_acts = pltpu.make_async_remote_copy(
        src_ref=hidden_ref.at[0, 1], dst_ref=acts_in.at[1],
        send_sem=pair_send.at[1], recv_sem=pair_recv.at[1],
        device_id=mirror, device_id_type=MESH,
    )

    sent = []

    def send(s, origin, way, condition):
        sent.append((s, origin, way, condition))
        when(condition, lambda: hop(s, origin, way).start())

    def send_own(s):
        send(s, k, LEFT, has_left)
        send(s, k, RIGHT, has_right)
        send(s, k, SIBLING, True)

    def relay(s, j):
        from_left = z >= j
        from_right = z + j < n
        left_origin = jnp.maximum(k - 2 * j, 0)
        right_origin = jnp.minimum(k + 2 * j, n_dp - 1)
        pl.when(from_left)(lambda: arrived(s, left_origin))
        send(s, left_origin, RIGHT, jnp.logical_and(from_left, has_right))
        send(s, left_origin, SIBLING, from_left)
        pl.when(from_right)(lambda: arrived(s, right_origin))
        send(s, right_origin, LEFT, jnp.logical_and(from_right, has_left))
        send(s, right_origin, SIBLING, from_right)

    mirror_rows.start()
    send_own(0)
    mirror_acts.start()
    arrived(1, k)
    send_own(1)
    for j in range(1, n - 1):
        relay(0, j)
        relay(1, j)

    at_token = lax.broadcasted_iota(jnp.int32, (tokens, tokens), 0)
    at_row = lax.broadcasted_iota(jnp.int32, (tokens, tokens), 1)
    slot, inside = at_token // (micro * group_rows), at_token % (micro * group_rows)
    of_micro, of_slot = inside // group_rows, inside % group_rows
    wanted = (
        slot * (micro * group_rows) + (of_slot // row_total) * block_rows
        + of_micro * row_total + of_slot % row_total
    )
    order = jnp.where(wanted == at_row, 1.0, 0.0).astype(jnp.bfloat16)

    load_acts.wait()
    mirror_acts.wait_recv()
    acts_ref[...] = lax.dot_general(
        acts_in[...].reshape(tokens, share), order,
        (((0,), (0,)), ((), ())), preferred_element_type=jnp.float32,
    ).astype(jnp.bfloat16)

    if n > 1:
        relay(0, n - 1)
        relay(1, n - 1)

    for s in range(2):
        arrived(s, sibling)
        for j in range(1, n):
            pl.when(z >= j)(functools.partial(arrived, s, jnp.maximum(sibling - 2 * j, 0)))
            pl.when(z + j < n)(functools.partial(arrived, s, jnp.minimum(sibling + 2 * j, n_dp - 1)))
        for h in range(2):
            blocks = [
                landed[s, rank].astype(jnp.float32)[h * block_rows:(h + 1) * block_rows]
                for rank in range(n_dp)
            ]
            rows_ref[pl.ds(s * (tokens // 2), tokens // 2), pl.ds(h * half, half)] = jnp.concatenate(
                blocks, axis=0
            ).astype(jnp.bfloat16)
    load_weight.wait()

    def give_back(c):
        columns = pl.ds(c * chunk, chunk)
        return pltpu.make_async_remote_copy(
            src_ref=ret.at[:, :, columns], dst_ref=out_ref.at[0, 1, :, :, columns],
            send_sem=ret_send.at[c], recv_sem=ret_recv.at[c],
            device_id=mirror, device_id_type=MESH,
        )

    for c in range(share // chunk):
        columns = pl.ds(c * chunk, chunk)
        product = lax.dot_general(
            weight_out[columns, :], rows_ref[...],
            (((1,), (1,)), ((), ())), preferred_element_type=jnp.float32,
        )
        rounded = (product * scale_factor).astype(jnp.bfloat16)
        value = lax.dot_general(
            order, rounded, (((1,), (1,)), ((), ())), preferred_element_type=jnp.float32
        ).astype(jnp.bfloat16).reshape(2, micro, group_rows, chunk)
        ret[:, :, columns] = value[1]
        give_back(c).start()
        out_ref[0, 0, :, :, columns] = value[0]

    mirror_rows.wait_send()
    mirror_acts.wait_send()
    for s, origin, way, condition in sent:
        when(condition, functools.partial(lambda *a: hop(*a).wait_send(), s, origin, way))
    for c in range(share // chunk):
        give_back(c).wait()


def update_kernel(
    factor, step, weight_ref, acts_ref, rows_ref, back_ref, new_ref, out_ref, slots, sems, out_sem
):
    put_back = pltpu.make_async_copy(back_ref, out_ref, out_sem)
    put_back.start()
    depth = slots.shape[0]
    steps = weight_ref.shape[1] // step

    def put(i):
        return pltpu.make_async_copy(
            slots.at[i % depth], new_ref.at[0, :, pl.ds(i * step, step)], sems.at[i % depth]
        )

    for i in range(steps):
        columns = pl.ds(i * step, step)
        if i >= depth:
            put(i - depth).wait()
        total = jnp.dot(acts_ref[...], rows_ref[:, columns], preferred_element_type=jnp.float32)
        slots[i % depth] = (
            weight_ref[:, columns].astype(jnp.float32) - factor * total
        ).astype(jnp.bfloat16)
        put(i).start()
    for i in range(max(0, steps - depth), steps):
        put(i).wait()
    put_back.wait()


def shards(n_pipe, n_dp, grad_out, hidden, weights, counts):
    _, _, micro, row_total, width = grad_out.shape
    group_rows, share = hidden.shape[3], hidden.shape[4]
    block = 2 * micro * row_total
    half = width // 2
    tokens = 2 * micro * group_rows
    scale_factor = float(width) ** (-0.5)
    chunk = 384 if share % 384 == 0 else share
    step = 256 if width % 256 == 0 else 128
    vmem = pl.BlockSpec(memory_space=pltpu.VMEM)
    hbm = pl.BlockSpec(memory_space=pltpu.HBM)
    rows, acts, weight, back = pl.pallas_call(
        functools.partial(gather_kernel, n_pipe, n_dp, scale_factor, chunk),
        out_shape=(
            jax.ShapeDtypeStruct((tokens, width), jnp.bfloat16),
            jax.ShapeDtypeStruct((share, tokens), jnp.bfloat16),
            jax.ShapeDtypeStruct((share, width), jnp.bfloat16),
            jax.ShapeDtypeStruct(hidden.shape, jnp.bfloat16),
        ),
        in_specs=[pl.BlockSpec(memory_space=pltpu.SMEM), hbm, hbm, hbm],
        out_specs=(vmem, vmem, vmem, vmem),
        scratch_shapes=[
            pltpu.VMEM((2, micro, row_total, width), jnp.bfloat16),
            pltpu.VMEM((2, block, half), jnp.float32),
            pltpu.VMEM((block, half), jnp.bfloat16),
            pltpu.VMEM((2, n_dp, block, half), jnp.bfloat16),
            pltpu.VMEM((2, micro, group_rows, share), jnp.bfloat16),
            pltpu.VMEM((micro, group_rows, share), jnp.bfloat16),
            pltpu.SemaphoreType.DMA((2, n_dp, 3)),
            pltpu.SemaphoreType.DMA((2, n_dp)),
            pltpu.SemaphoreType.DMA((2,)),
            pltpu.SemaphoreType.DMA((2,)),
            pltpu.SemaphoreType.DMA((share // chunk,)),
            pltpu.SemaphoreType.DMA((share // chunk,)),
            pltpu.SemaphoreType.DMA((3,)),
        ],
        compiler_params=pltpu.CompilerParams(
            collective_id=0, has_side_effects=True, vmem_limit_bytes=42 * 2**20
        ),
        name="gather",
    )(counts.reshape(2, micro), grad_out, hidden, weights)
    new_weights, grad_hidden = pl.pallas_call(
        functools.partial(update_kernel, step_rate * scale_factor, step),
        out_shape=(
            jax.ShapeDtypeStruct(weights.shape, jnp.bfloat16),
            jax.ShapeDtypeStruct(hidden.shape, jnp.bfloat16),
        ),
        in_specs=[vmem, vmem, vmem, vmem],
        out_specs=(hbm, hbm),
        scratch_shapes=[
            pltpu.VMEM((4, share, step), jnp.bfloat16),
            pltpu.SemaphoreType.DMA((4,)),
            pltpu.SemaphoreType.DMA,
        ],
        compiler_params=pltpu.CompilerParams(vmem_limit_bytes=24 * 2**20),
        name="update",
    )(weight, acts, rows, back)
    return grad_hidden, new_weights


def solution(mesh):
    return jax.shard_map(
        functools.partial(shards, mesh.shape["pipe"], mesh.shape["dp"]),
        mesh=mesh,
        in_specs=(
            P("pipe", None, None, "dp", None),
            P("pipe", None, None, None, "dp"),
            P("pipe", "dp", None),
            P("pipe", None, None, "dp"),
        ),
        out_specs=(P("pipe", None, None, None, "dp"), P("pipe", "dp", None)),
        check_vma=False,
    )
```

time: 41.3 us -> 38.9 us (0.942)
  local copies, waits for them, and re-layouts: 6.69 us -> 2.53 us
  Pallas kernels: 33.7 us -> 35.5 us
    unnamed x8 -> x6, local copies, waits for them, and re-layouts: 6.69 us -> 2.53 us
    pallas_call x1, Pallas kernels: 5.53 us -> 6.55 us  [shards(): pl.pallas_call(functools.partial(update_kernel, step_rate * scale_factor,...]
    pallas_call x1, Pallas kernels: 28.2 us -> 28.9 us  [shards(): pl.pallas_call(functools.partial(gather_kernel, n_pipe, n_dp, scale_facto...]
where the time goes in v2:
time: 38.9 us; the launch traced here: 38.7 us
  Pallas kernels  35.5 us (91%)
  local copies, waits for them, and re-layouts  2.53 us (7%)
  between operations  0.65 us (2%)
    pallas_call x1, Pallas kernels, shards(): pl.pallas_call(functools.partial(gather_kernel, n_pipe, n_dp, scale_facto...  28.9 us
    pallas_call x1, Pallas kernels, shards(): pl.pallas_call(functools.partial(update_kernel, step_rate * scale_factor,...  6.55 us
    unnamed x6, local copies, waits for them, and re-layouts  2.53 us

profile of v2, /device:TPU:0, one launch (start us, length us, event | category | flops | bytes accessed | tf_op | source)
XLA Modules:
  0.0 38.7 jit_solution(14223394807597951252)
XLA Ops:
  0.6 0.0 copy-start
  0.6 1.0 %copy-done = bf16[1,2,2,32,1152]{4,3,2,1,0:T(8,128)(2,1)S(1)} copy-done((bf16[1,2,2,32,1152]{4,3,2,1,0:T(8,128)(2,1)S(1)}, bf16[1,2,2,32,1152]{4,3,2,1,0:T(8,128)(2,1)}, u32[]{:S(2)}) %copy-start) | copy-done | bytes 294936
  1.6 0.0 copy-start.1
  1.6 0.9 %copy-done.1 = bf16[1,2,2,4,3584]{4,3,2,1,0:T(4,128)(2,1)S(1)} copy-done((bf16[1,2,2,4,3584]{4,3,2,1,0:T(4,128)(2,1)S(1)}, bf16[1,2,2,4,3584]{4,3,2,1,0:T(4,128)(2,1)}, u32[]{:S(2)}) %copy-start.1) | copy-done | bytes 114712
  2.5 0.0 copy-start.2
  2.5 0.7 %copy-done.2 = s32[1,2,2,1]{2,3,1,0:T(1,128)S(1)} copy-done((s32[1,2,2,1]{2,3,1,0:T(1,128)S(1)}, s32[1,2,2,1]{2,3,1,0:T(1,128)}, u32[]{:S(2)}) %copy-start.2) | copy-done | bytes 40
  3.2 28.9 %gather.1 = (bf16[128,3584]{1,0:T(8,128)(2,1)S(1)}, bf16[1152,128]{1,0:T(8,128)(2,1)S(1)}, bf16[1152,3584]{1,0:T(8,128)(2,1)S(1)}, bf16[1,2,2,32,1152]{4,3,2,1,0:T(8,128)(2,1)S(1)}) custom-call(s32[2,2]{1,0:T(2,128)S(1)} %bitcast.1, bf16[1,2,2,4,3584]{4,3,2,1,0:T(4,128)(2,1)S(1)} %copy-done.1, bf16[1,2,2,32,1152]{4,3,2,1,0:T(8,128)(2,1)S(1)} %copy-done, ...), custom_call_target="tpu_custom_call" | custom-call | tf_op jit(solution)/shard_map/gather/pallas_call | solution.py:240
  32.1 6.5 %update.1 = (bf16[1,1152,3584]{2,1,0:T(8,128)(2,1)}, bf16[1,2,2,32,1152]{4,3,2,1,0:T(8,128)(2,1)}) custom-call(bf16[1152,3584]{1,0:T(8,128)(2,1)S(1)} %get-tuple-element.8.weight_ref, bf16[1152,128]{1,0:T(8,128)(2,1)S(1)} %get-tuple-element.9.acts_ref, bf16[128,3584]{1,0:T(8,128)(2,1)S(1)} %get-tuple-element.10.rows_ref, ...), custom_call_target="tpu_custom_call" | custom-call | tf_op jit(solution)/shard_map/update/pallas_call | solution.py:270
Async XLA Ops:
  0.6 1.0 %copy-start = (bf16[1,2,2,32,1152]{4,3,2,1,0:T(8,128)(2,1)S(1)}, bf16[1,2,2,32,1152]{4,3,2,1,0:T(8,128)(2,1)}, u32[]{:S(2)}) copy-start(bf16[1,2,2,32,1152]{4,3,2,1,0:T(8,128)(2,1)} %hidden_ref.1) | copy-start | bytes 884740
  1.6 0.9 %copy-start.1 = (bf16[1,2,2,4,3584]{4,3,2,1,0:T(4,128)(2,1)S(1)}, bf16[1,2,2,4,3584]{4,3,2,1,0:T(4,128)(2,1)}, u32[]{:S(2)}) copy-start(bf16[1,2,2,4,3584]{4,3,2,1,0:T(4,128)(2,1)} %grad_ref.1) | copy-start | bytes 344068
  2.5 0.7 %copy-start.2 = (s32[1,2,2,1]{2,3,1,0:T(1,128)S(1)}, s32[1,2,2,1]{2,3,1,0:T(1,128)}, u32[]{:S(2)}) copy-start(s32[1,2,2,1]{2,3,1,0:T(1,128)} %param.7) | copy-start | bytes 52

commit v3 on v2

--- a/solution.py
+++ b/solution.py
@@ -19,8 +19,22 @@
         pl.when(condition)(action)
 
 
+def update_rows(factor, weight_ref, acts_ref, rows_ref, target_ref, first, count, target_first):
+    high = 192 if count % 192 == 0 else count
+    wide = 256 if weight_ref.shape[1] % 256 == 0 else 128
+    for r in range(0, count, high):
+        for c in range(0, weight_ref.shape[1], wide):
+            columns = pl.ds(c, wide)
+            total = jnp.dot(
+                acts_ref[pl.ds(first + r, high), :], rows_ref[:, columns], preferred_element_type=jnp.float32
+            )
+            target_ref[pl.ds(target_first + r, high), columns] = (
+                weight_ref[pl.ds(first + r, high), columns].astype(jnp.float32) - factor * total
+            ).astype(jnp.bfloat16)
+
+
 def gather_kernel(
-    n_pipe, n_dp, scale_factor, chunk,
+    n_pipe, n_dp, scale_factor, chunk, early,
     counts_ref, grad_ref, hidden_ref, weights_ref,
     rows_ref, acts_ref, weight_out, out_ref,
     own_grad, staged, own_slot1, landed, acts_in, ret,
@@ -191,6 +205,8 @@
         give_back(c).start()
         out_ref[0, 0, :, :, columns] = value[0]
 
+    update_rows(step_rate * scale_factor, weight_out, acts_ref, rows_ref, weight_out, 0, early, 0)
+
     mirror_rows.wait_send()
     mirror_acts.wait_send()
     for s, origin, way, condition in sent:
@@ -200,28 +216,23 @@
 
 
 def update_kernel(
-    factor, step, weight_ref, acts_ref, rows_ref, back_ref, new_ref, out_ref, slots, sems, out_sem
+    factor, early, step, weight_ref, acts_ref, rows_ref, back_ref, new_ref, out_ref, late, sems, out_sem
 ):
     put_back = pltpu.make_async_copy(back_ref, out_ref, out_sem)
+    share = weight_ref.shape[0]
+
+    def put(i):
+        first = i * step
+        source = weight_ref.at[pl.ds(first, step)] if first < early else late.at[pl.ds(first - early, step)]
+        return pltpu.make_async_copy(source, new_ref.at[0, pl.ds(first, step)], sems.at[i])
+
+    for i in range(early // step):
+        put(i).start()
     put_back.start()
-    depth = slots.shape[0]
-    steps = weight_ref.shape[1] // step
-
-    def put(i):
-        return pltpu.make_async_copy(
-            slots.at[i % depth], new_ref.at[0, :, pl.ds(i * step, step)], sems.at[i % depth]
-        )
-
-    for i in range(steps):
-        columns = pl.ds(i * step, step)
-        if i >= depth:
-            put(i - depth).wait()
-        total = jnp.dot(acts_ref[...], rows_ref[:, columns], preferred_element_type=jnp.float32)
-        slots[i % depth] = (
-            weight_ref[:, columns].astype(jnp.float32) - factor * total
-        ).astype(jnp.bfloat16)
+    for i in range(early // step, share // step):
+        update_rows(factor, weight_ref, acts_ref, rows_ref, late, i * step, step, i * step - early)
         put(i).start()
-    for i in range(max(0, steps - depth), steps):
+    for i in range(share // step):
         put(i).wait()
     put_back.wait()
 
@@ -234,11 +245,12 @@
     tokens = 2 * micro * group_rows
     scale_factor = float(width) ** (-0.5)
     chunk = 384 if share % 384 == 0 else share
-    step = 256 if width % 256 == 0 else 128
+    early = 2 * (share // chunk) // 3 * chunk
+    step = 192 if chunk % 192 == 0 else chunk
     vmem = pl.BlockSpec(memory_space=pltpu.VMEM)
     hbm = pl.BlockSpec(memory_space=pltpu.HBM)
     rows, acts, weight, back = pl.pallas_call(
-        functools.partial(gather_kernel, n_pipe, n_dp, scale_factor, chunk),
+        functools.partial(gather_kernel, n_pipe, n_dp, scale_factor, chunk, early),
         out_shape=(
             jax.ShapeDtypeStruct((tokens, width), jnp.bfloat16),
             jax.ShapeDtypeStruct((share, tokens), jnp.bfloat16),
@@ -268,7 +280,7 @@
         name="gather",
     )(counts.reshape(2, micro), grad_out, hidden, weights)
     new_weights, grad_hidden = pl.pallas_call(
-        functools.partial(update_kernel, step_rate * scale_factor, step),
+        functools.partial(update_kernel, step_rate * scale_factor, early, step),
         out_shape=(
             jax.ShapeDtypeStruct(weights.shape, jnp.bfloat16),
             jax.ShapeDtypeStruct(hidden.shape, jnp.bfloat16),
@@ -276,8 +288,8 @@
         in_specs=[vmem, vmem, vmem, vmem],
         out_specs=(hbm, hbm),
         scratch_shapes=[
-            pltpu.VMEM((4, share, step), jnp.bfloat16),
-            pltpu.SemaphoreType.DMA((4,)),
+            pltpu.VMEM((share - early, width), jnp.bfloat16),
+            pltpu.SemaphoreType.DMA((share // step,)),
             pltpu.SemaphoreType.DMA,
         ],
         compiler_params=pltpu.CompilerParams(vmem_limit_bytes=24 * 2**20),

time: 38.9 us -> 36.4 us (0.936)
  Pallas kernels: 35.5 us -> 33 us
    pallas_call x1, Pallas kernels: 6.55 us -> 3.47 us  [shards(): pl.pallas_call(functools.partial(update_kernel, step_rate * scale_factor,...]
    pallas_call x1, Pallas kernels: 28.9 us -> 29.5 us  [shards(): pl.pallas_call(functools.partial(gather_kernel, n_pipe, n_dp, scale_facto...]
where the time goes in v3:
time: 36.4 us; the launch traced here: 36.2 us
  Pallas kernels  33 us (91%)
  local copies, waits for them, and re-layouts  2.53 us (7%)
  between operations  0.65 us (2%)
    pallas_call x1, Pallas kernels, shards(): pl.pallas_call(functools.partial(gather_kernel, n_pipe, n_dp, scale_facto...  29.5 us
    pallas_call x1, Pallas kernels, shards(): pl.pallas_call(functools.partial(update_kernel, step_rate * scale_factor,...  3.47 us
    unnamed x6, local copies, waits for them, and re-layouts  2.53 us

profile of v3, /device:TPU:0, one launch (start us, length us, event | category | flops | bytes accessed | tf_op | source)
XLA Modules:
  0.0 36.2 jit_solution(16578600259112115411)
XLA Ops:
  0.6 0.0 copy-start
  0.6 1.0 %copy-done = bf16[1,2,2,32,1152]{4,3,2,1,0:T(8,128)(2,1)S(1)} copy-done((bf16[1,2,2,32,1152]{4,3,2,1,0:T(8,128)(2,1)S(1)}, bf16[1,2,2,32,1152]{4,3,2,1,0:T(8,128)(2,1)}, u32[]{:S(2)}) %copy-start) | copy-done | bytes 294936
  1.6 0.0 copy-start.1
  1.6 0.9 %copy-done.1 = bf16[1,2,2,4,3584]{4,3,2,1,0:T(4,128)(2,1)S(1)} copy-done((bf16[1,2,2,4,3584]{4,3,2,1,0:T(4,128)(2,1)S(1)}, bf16[1,2,2,4,3584]{4,3,2,1,0:T(4,128)(2,1)}, u32[]{:S(2)}) %copy-start.1) | copy-done | bytes 114712
  2.5 0.0 copy-start.2
  2.5 0.7 %copy-done.2 = s32[1,2,2,1]{2,3,1,0:T(1,128)S(1)} copy-done((s32[1,2,2,1]{2,3,1,0:T(1,128)S(1)}, s32[1,2,2,1]{2,3,1,0:T(1,128)}, u32[]{:S(2)}) %copy-start.2) | copy-done | bytes 40
  3.2 29.5 %gather.1 = (bf16[128,3584]{1,0:T(8,128)(2,1)S(1)}, bf16[1152,128]{1,0:T(8,128)(2,1)S(1)}, bf16[1152,3584]{1,0:T(8,128)(2,1)S(1)}, bf16[1,2,2,32,1152]{4,3,2,1,0:T(8,128)(2,1)S(1)}) custom-call(s32[2,2]{1,0:T(2,128)S(1)} %bitcast.1, bf16[1,2,2,4,3584]{4,3,2,1,0:T(4,128)(2,1)S(1)} %copy-done.1, bf16[1,2,2,32,1152]{4,3,2,1,0:T(8,128)(2,1)S(1)} %copy-done, ...), custom_call_target="tpu_custom_call" | custom-call | tf_op jit(solution)/shard_map/gather/pallas_call | solution.py:252
  32.7 3.5 %update.1 = (bf16[1,1152,3584]{2,1,0:T(8,128)(2,1)}, bf16[1,2,2,32,1152]{4,3,2,1,0:T(8,128)(2,1)}) custom-call(bf16[1152,3584]{1,0:T(8,128)(2,1)S(1)} %get-tuple-element.8.weight_ref, bf16[1152,128]{1,0:T(8,128)(2,1)S(1)} %get-tuple-element.9.acts_ref, bf16[128,3584]{1,0:T(8,128)(2,1)S(1)} %get-tuple-element.10.rows_ref, ...), custom_call_target="tpu_custom_call" | custom-call | tf_op jit(solution)/shard_map/update/pallas_call | solution.py:282
Async XLA Ops:
  0.6 1.0 %copy-start = (bf16[1,2,2,32,1152]{4,3,2,1,0:T(8,128)(2,1)S(1)}, bf16[1,2,2,32,1152]{4,3,2,1,0:T(8,128)(2,1)}, u32[]{:S(2)}) copy-start(bf16[1,2,2,32,1152]{4,3,2,1,0:T(8,128)(2,1)} %hidden_ref.1) | copy-start | bytes 884740
  1.6 0.9 %copy-start.1 = (bf16[1,2,2,4,3584]{4,3,2,1,0:T(4,128)(2,1)S(1)}, bf16[1,2,2,4,3584]{4,3,2,1,0:T(4,128)(2,1)}, u32[]{:S(2)}) copy-start(bf16[1,2,2,4,3584]{4,3,2,1,0:T(4,128)(2,1)} %grad_ref.1) | copy-start | bytes 344068
  2.5 0.7 %copy-start.2 = (s32[1,2,2,1]{2,3,1,0:T(1,128)S(1)}, s32[1,2,2,1]{2,3,1,0:T(1,128)}, u32[]{:S(2)}) copy-start(s32[1,2,2,1]{2,3,1,0:T(1,128)} %param.7) | copy-start | bytes 52

commit v4 on v3

--- a/solution.py
+++ b/solution.py
@@ -138,12 +138,18 @@
         send(s, right_origin, LEFT, jnp.logical_and(from_right, has_left))
         send(s, right_origin, SIBLING, from_right)
 
+    def drain():
+        for s, origin, way, condition in sent:
+            when(condition, functools.partial(lambda *a: hop(*a).wait_send(), s, origin, way))
+        sent.clear()
+
     mirror_rows.start()
     send_own(0)
-    mirror_acts.start()
     arrived(1, k)
     send_own(1)
+    mirror_acts.start()
     for j in range(1, n - 1):
+        drain()
         relay(0, j)
         relay(1, j)
 
@@ -165,8 +171,8 @@
     ).astype(jnp.bfloat16)
 
     if n > 1:
+        relay(1, n - 1)
         relay(0, n - 1)
-        relay(1, n - 1)
 
     for s in range(2):
         arrived(s, sibling)
@@ -209,8 +215,7 @@
 
     mirror_rows.wait_send()
     mirror_acts.wait_send()
-    for s, origin, way, condition in sent:
-        when(condition, functools.partial(lambda *a: hop(*a).wait_send(), s, origin, way))
+    drain()
     for c in range(share // chunk):
         give_back(c).wait()
 
@@ -278,7 +283,7 @@
             collective_id=0, has_side_effects=True, vmem_limit_bytes=42 * 2**20
         ),
         name="gather",
-    )(counts.reshape(2, micro), grad_out, hidden, weights)
+    )(*[pltpu.with_memory_space_constraint(x, pltpu.HBM) for x in (counts.reshape(2, micro), grad_out, hidden, weights)])
     new_weights, grad_hidden = pl.pallas_call(
         functools.partial(update_kernel, step_rate * scale_factor, early, step),
         out_shape=(

time: 36.4 us -> 33.1 us (0.909)
  local copies, waits for them, and re-layouts: 2.53 us -> 0 us
  Pallas kernels: 33 us -> 32.3 us
    unnamed x6 -> x0, local copies, waits for them, and re-layouts: 2.53 us -> none
    pallas_call x1, Pallas kernels: 29.5 us -> 28.8 us  [shards(): pl.pallas_call(functools.partial(gather_kernel, n_pipe, n_dp, scale_facto...]
where the time goes in v4:
time: 33.1 us; the launch traced here: 32.9 us
  Pallas kernels  32.3 us (98%)
  between operations  0.64 us (2%)
    pallas_call x1, Pallas kernels, shards(): pl.pallas_call(functools.partial(gather_kernel, n_pipe, n_dp, scale_facto...  28.8 us
    pallas_call x1, Pallas kernels, shards(): pl.pallas_call(functools.partial(update_kernel, step_rate * scale_factor,...  3.47 us

profile of v4, /device:TPU:0, one launch (start us, length us, event | category | flops | bytes accessed | tf_op | source)
XLA Modules:
  0.0 32.9 jit_solution(15449651581944220050)
XLA Ops:
  0.6 28.8 %gather.1 = (bf16[128,3584]{1,0:T(8,128)(2,1)S(1)}, bf16[1152,128]{1,0:T(8,128)(2,1)S(1)}, bf16[1152,3584]{1,0:T(8,128)(2,1)S(1)}, bf16[1,2,2,32,1152]{4,3,2,1,0:T(8,128)(2,1)S(1)}) custom-call(s32[2,2]{1,0:T(2,128)} %bitcast.1, bf16[1,2,2,4,3584]{4,3,2,1,0:T(4,128)(2,1)} %grad_ref.1, bf16[1,2,2,32,1152]{4,3,2,1,0:T(8,128)(2,1)} %hidden_ref.1, ...), custom_call_target="tpu_custom_call" | custom-call | tf_op jit(solution)/shard_map/gather/pallas_call | solution.py:257
  29.5 3.5 %update.1 = (bf16[1,1152,3584]{2,1,0:T(8,128)(2,1)}, bf16[1,2,2,32,1152]{4,3,2,1,0:T(8,128)(2,1)}) custom-call(bf16[1152,3584]{1,0:T(8,128)(2,1)S(1)} %get-tuple-element.8.weight_ref, bf16[1152,128]{1,0:T(8,128)(2,1)S(1)} %get-tuple-element.9.acts_ref, bf16[128,3584]{1,0:T(8,128)(2,1)S(1)} %get-tuple-element.10.rows_ref, ...), custom_call_target="tpu_custom_call" | custom-call | tf_op jit(solution)/shard_map/update/pallas_call | solution.py:287

commit v5 on v4

--- a/solution.py
+++ b/solution.py
@@ -90,63 +90,74 @@
 
     pl.semaphore_wait(barrier, 2 + has_left.astype(jnp.int32) + has_right.astype(jnp.int32))
 
-    def hop(s, origin, way):
+    cuts = (1, 2 if half % 256 == 0 else 1)
+
+    def cut(s, part):
+        return pl.ds(part * (half // cuts[s]), half // cuts[s])
+
+    def hop(s, part, origin, way):
         target = {LEFT: k - 2, RIGHT: k + 2, SIBLING: sibling}[way]
         return pltpu.make_async_remote_copy(
-            src_ref=landed.at[s, origin],
-            dst_ref=landed.at[s, origin],
-            send_sem=send_sem.at[s, origin, way],
-            recv_sem=recv_sem.at[s, origin],
+            src_ref=landed.at[s, origin, :, cut(s, part)],
+            dst_ref=landed.at[s, origin, :, cut(s, part)],
+            send_sem=send_sem.at[s, part, origin, way],
+            recv_sem=recv_sem.at[s, part, origin],
             device_id=(p, target),
             device_id_type=MESH,
         )
 
-    def arrived(s, origin):
-        hop(s, origin, SIBLING).wait_recv()
-
-    mirror_rows = pltpu.make_async_remote_copy(
-        src_ref=own_slot1, dst_ref=landed.at[1, k],
-        send_sem=pair_send.at[0], recv_sem=recv_sem.at[1, k],
+    def arrived(s, part, origin):
+        hop(s, part, origin, SIBLING).wait_recv()
+
+    mirror_rows = [
+        pltpu.make_async_remote_copy(
+            src_ref=own_slot1.at[:, cut(1, part)], dst_ref=landed.at[1, k, :, cut(1, part)],
+            send_sem=pair_send.at[1 + part], recv_sem=recv_sem.at[1, part, k],
+            device_id=mirror, device_id_type=MESH,
+        )
+        for part in range(cuts[1])
+    ]
+    mirror_acts = pltpu.make_async_remote_copy(
+        src_ref=hidden_ref.at[0, 1], dst_ref=acts_in.at[1],
+        send_sem=pair_send.at[0], recv_sem=pair_recv.at[0],
         device_id=mirror, device_id_type=MESH,
     )
-    mirror_acts = pltpu.make_async_remote_copy(
-        src_ref=hidden_ref.at[0, 1], dst_ref=acts_in.at[1],
-        send_sem=pair_send.at[1], recv_sem=pair_recv.at[1],
-        device_id=mirror, device_id_type=MESH,
-    )
 
     sent = []
 
-    def send(s, origin, way, condition):
-        sent.append((s, origin, way, condition))
-        when(condition, lambda: hop(s, origin, way).start())
-
-    def send_own(s):
-        send(s, k, LEFT, has_left)
-        send(s, k, RIGHT, has_right)
-        send(s, k, SIBLING, True)
+    def send(s, part, origin, way, condition):
+        sent.append((s, part, origin, way, condition))
+        when(condition, lambda: hop(s, part, origin, way).start())
+
+    def send_own(s, part):
+        send(s, part, k, LEFT, has_left)
+        send(s, part, k, RIGHT, has_right)
+        send(s, part, k, SIBLING, True)
 
     def relay(s, j):
         from_left = z >= j
         from_right = z + j < n
         left_origin = jnp.maximum(k - 2 * j, 0)
         right_origin = jnp.minimum(k + 2 * j, n_dp - 1)
-        pl.when(from_left)(lambda: arrived(s, left_origin))
-        send(s, left_origin, RIGHT, jnp.logical_and(from_left, has_right))
-        send(s, left_origin, SIBLING, from_left)
-        pl.when(from_right)(lambda: arrived(s, right_origin))
-        send(s, right_origin, LEFT, jnp.logical_and(from_right, has_left))
-        send(s, right_origin, SIBLING, from_right)
+        for part in range(cuts[s]):
+            pl.when(from_left)(functools.partial(arrived, s, part, left_origin))
+            send(s, part, left_origin, RIGHT, jnp.logical_and(from_left, has_right))
+            send(s, part, left_origin, SIBLING, from_left)
+            pl.when(from_right)(functools.partial(arrived, s, part, right_origin))
+            send(s, part, right_origin, LEFT, jnp.logical_and(from_right, has_left))
+            send(s, part, right_origin, SIBLING, from_right)
 
     def drain():
-        for s, origin, way, condition in sent:
-            when(condition, functools.partial(lambda *a: hop(*a).wait_send(), s, origin, way))
+        for s, part, origin, way, condition in sent:
+            when(condition, functools.partial(lambda *a: hop(*a).wait_send(), s, part, origin, way))
         sent.clear()
 
-    mirror_rows.start()
-    send_own(0)
-    arrived(1, k)
-    send_own(1)
+    for copy in mirror_rows:
+        copy.start()
+    send_own(0, 0)
+    for part in range(cuts[1]):
+        arrived(1, part, k)
+        send_own(1, part)
     mirror_acts.start()
     for j in range(1, n - 1):
         drain()
@@ -175,10 +186,13 @@
         relay(0, n - 1)
 
     for s in range(2):
-        arrived(s, sibling)
-        for j in range(1, n):
-            pl.when(z >= j)(functools.partial(arrived, s, jnp.maximum(sibling - 2 * j, 0)))
-            pl.when(z + j < n)(functools.partial(arrived, s, jnp.minimum(sibling + 2 * j, n_dp - 1)))
+        for part in range(cuts[s]):
+            arrived(s, part, sibling)
+            for j in range(1, n):
+                pl.when(z >= j)(functools.partial(arrived, s, part, jnp.maximum(sibling - 2 * j, 0)))
+                pl.when(z + j < n)(
+                    functools.partial(arrived, s, part, jnp.minimum(sibling + 2 * j, n_dp - 1))
+                )
         for h in range(2):
             blocks = [
                 landed[s, rank].astype(jnp.float32)[h * block_rows:(h + 1) * block_rows]
@@ -213,7 +227,8 @@
 
     update_rows(step_rate * scale_factor, weight_out, acts_ref, rows_ref, weight_out, 0, early, 0)
 
-    mirror_rows.wait_send()
+    for copy in mirror_rows:
+        copy.wait_send()
     mirror_acts.wait_send()
     drain()
     for c in range(share // chunk):
@@ -271,10 +286,10 @@
             pltpu.VMEM((2, n_dp, block, half), jnp.bfloat16),
             pltpu.VMEM((2, micro, group_rows, share), jnp.bfloat16),
             pltpu.VMEM((micro, group_rows, share), jnp.bfloat16),
-            pltpu.SemaphoreType.DMA((2, n_dp, 3)),
-            pltpu.SemaphoreType.DMA((2, n_dp)),
-            pltpu.SemaphoreType.DMA((2,)),
-            pltpu.SemaphoreType.DMA((2,)),
+            pltpu.SemaphoreType.DMA((2, 2, n_dp, 3)),
+            pltpu.SemaphoreType.DMA((2, 2, n_dp)),
+            pltpu.SemaphoreType.DMA((3,)),
+            pltpu.SemaphoreType.DMA((1,)),
             pltpu.SemaphoreType.DMA((share // chunk,)),
             pltpu.SemaphoreType.DMA((share // chunk,)),
             pltpu.SemaphoreType.DMA((3,)),

time: 33.1 us -> 32.7 us (0.988)
  Pallas kernels: 32.3 us -> 31.9 us
    pallas_call x1, Pallas kernels: 28.8 us -> 28.5 us  [shards(): pl.pallas_call(functools.partial(gather_kernel, n_pipe, n_dp, scale_facto...]
where the time goes in v5:
time: 32.7 us; the launch traced here: 32.6 us
  Pallas kernels  31.9 us (98%)
  between operations  0.64 us (2%)
    pallas_call x1, Pallas kernels, shards(): pl.pallas_call(functools.partial(gather_kernel, n_pipe, n_dp, scale_facto...  28.5 us
    pallas_call x1, Pallas kernels, shards(): pl.pallas_call(functools.partial(update_kernel, step_rate * scale_factor,...  3.47 us

profile of v5, /device:TPU:0, one launch (start us, length us, event | category | flops | bytes accessed | tf_op | source)
XLA Modules:
  0.0 32.6 jit_solution(146193470656316995)
XLA Ops:
  0.6 28.5 %gather.1 = (bf16[128,3584]{1,0:T(8,128)(2,1)S(1)}, bf16[1152,128]{1,0:T(8,128)(2,1)S(1)}, bf16[1152,3584]{1,0:T(8,128)(2,1)S(1)}, bf16[1,2,2,32,1152]{4,3,2,1,0:T(8,128)(2,1)S(1)}) custom-call(s32[2,2]{1,0:T(2,128)} %bitcast.1, bf16[1,2,2,4,3584]{4,3,2,1,0:T(4,128)(2,1)} %grad_ref.1, bf16[1,2,2,32,1152]{4,3,2,1,0:T(8,128)(2,1)} %hidden_ref.1, ...), custom_call_target="tpu_custom_call" | custom-call | tf_op jit(solution)/shard_map/gather/pallas_call | solution.py:272
  29.1 3.5 %update.1 = (bf16[1,1152,3584]{2,1,0:T(8,128)(2,1)}, bf16[1,2,2,32,1152]{4,3,2,1,0:T(8,128)(2,1)}) custom-call(bf16[1152,3584]{1,0:T(8,128)(2,1)S(1)} %get-tuple-element.8.weight_ref, bf16[1152,128]{1,0:T(8,128)(2,1)S(1)} %get-tuple-element.9.acts_ref, bf16[128,3584]{1,0:T(8,128)(2,1)S(1)} %get-tuple-element.10.rows_ref, ...), custom_call_target="tpu_custom_call" | custom-call | tf_op jit(solution)/shard_map/update/pallas_call | solution.py:302
